TPU v7x, 32 devices: a whole 2x2x4 slice. The times are simulated.
32 devices in a mesh: expert: 4 (over y, x), hidden: 8 (over z, core).
Axes of the slice: x: 2, y: 2, z: 4, core: 2. Of those that a mesh axis runs over, the one named last changes fastest.
Arguments:
- layer_input: bfloat16 [1024, 4096], P('expert', 'hidden'), may hold values from -6 to 6
- output_grad: bfloat16 [1024, 4096], P('expert', 'hidden'), may hold values from -1.5 to 1.5
- latent_saved: bfloat16 [1024, 1024], P('expert'), may hold values from -6 to 6
- combined_saved: bfloat16 [1024, 1024], P('expert'), may hold values from -6 to 6
- expert_ids: int32 [1024, 22], P('expert'), may hold values from 0 to 511, as said below
- gate_values: bfloat16 [1024, 22], P('expert'), may hold values from 0.099609375 to 1.5
- down_proj: bfloat16 [1024, 4096], P(None, 'hidden'), may hold values from -0.09375 to 0.09375
- up_proj: bfloat16 [1024, 4096], P(None, 'hidden'), may hold values from -0.1875 to 0.1875
- expert_in: bfloat16 [4, 1024, 2688], P('expert', None, 'hidden'), may hold values from -0.1875 to 0.1875
- expert_out: bfloat16 [4, 2688, 1024], P('expert', 'hidden'), may hold values from -0.125 to 0.125
Outputs:
- input_grad: bfloat16 [1024, 4096], P('expert', 'hidden')
- down_grad: float32 [1024, 4096], P('expert', 'hidden')
- up_grad: float32 [1024, 4096], P('expert', 'hidden')
- gate_grad: float32 [1024, 22], P('expert')
- expert_in_grad: float32 [4, 1024, 2688], P('expert', None, 'hidden')
- expert_out_grad: float32 [4, 2688, 1024], P('expert', 'hidden')
Inputs may be any that keep to these rules, and one draw needn't show every extreme that they name: `expert_ids`: each row names 22 different experts. In each aligned block of 256 rows (the rows of one index of the expert axis) each expert below 4 is named by at most 24 rows; some expert below 4 is named by exactly 24 rows in every block.
All inputs are finite; a program needn't handle non-finite values.
Results may differ from a plain program's by a relative error of at most 0.0065.
Values may be sent and summed in bfloat16 or wider, within the bound.
A program may use at most 64 MiB of HBM per device.

v0:
```python
import jax
import jax.numpy as jnp
from jax import lax
from jax.sharding import PartitionSpec as P


def slot_layout(table, groups, local_count):
    tokens_here = table.shape[0]
    return table.T.reshape(groups, local_count, tokens_here).transpose(1, 0, 2)[:, :, None, :]


def on_device(
    layer_input,
    output_grad,
    latent_saved,
    combined_saved,
    expert_ids,
    gate_values,
    down_proj,
    up_proj,
    expert_in,
    expert_out,
):
    groups = lax.axis_size("expert")
    shares = lax.axis_size("hidden")
    tokens_here = layer_input.shape[0]
    latent_width = latent_saved.shape[1]
    local_count = expert_in.shape[0]
    capacity = tokens_here * 3 // 32
    live_count = local_count * groups
    slot_total = local_count * groups * capacity
    part_width = latent_width // shares
    partial_cot = jnp.einsum("td,ld->tl", output_grad, up_proj, preferred_element_type=jnp.float32)
    member = expert_ids[:, :, None] == jnp.arange(live_count, dtype=jnp.int32)[None, None, :]
    per_token = jnp.sum(member.astype(jnp.int32), axis=1)
    before = jnp.cumsum(per_token, axis=0) - per_token
    gate_token = jnp.sum(
        jnp.where(member, gate_values.astype(jnp.float32)[:, :, None], 0.0), axis=1
    )
    rank_iota = jnp.arange(capacity, dtype=jnp.int32)[None, None, :, None]
    hit_slot = (slot_layout(per_token, groups, local_count) == 1) & (
        slot_layout(before, groups, local_count) == rank_iota
    )
    gate_slot = jnp.sum(
        jnp.where(hit_slot, slot_layout(gate_token, groups, local_count), 0.0), axis=3
    )
    gate_send = gate_slot.astype(jnp.bfloat16)
    dispatch_bf = hit_slot.astype(jnp.bfloat16).reshape(slot_total, tokens_here)
    cot_part = lax.psum_scatter(partial_cot, "hidden", scatter_dimension=1, tiled=True).astype(
        jnp.bfloat16
    )
    latent_part = lax.dynamic_slice_in_dim(
        latent_saved, lax.axis_index("hidden") * part_width, part_width, 1
    )
    cot_rows = jnp.dot(dispatch_bf, cot_part, preferred_element_type=jnp.float32).astype(
        jnp.bfloat16
    )
    latent_rows = jnp.dot(dispatch_bf, latent_part, preferred_element_type=jnp.float32).astype(
        jnp.bfloat16
    )
    cot_piece, latent_piece, gate_recv = (
        lax.all_to_all(
            cot_rows.reshape(local_count, groups, capacity, part_width),
            "expert",
            split_axis=1,
            concat_axis=1,
            tiled=True,
        ),
        lax.all_to_all(
            latent_rows.reshape(local_count, groups, capacity, part_width),
            "expert",
            split_axis=1,
            concat_axis=1,
            tiled=True,
        ),
        lax.all_to_all(gate_send, "expert", split_axis=1, concat_axis=1, tiled=True),
    )
    cot_recv, latent_recv = (
        lax.all_gather(cot_piece, "hidden", axis=3, tiled=True),
        lax.all_gather(latent_piece, "hidden", axis=3, tiled=True),
    )
    row_count = groups * capacity
    cot_block = cot_recv.reshape(local_count, row_count, latent_width)
    latent_block = latent_recv.reshape(local_count, row_count, latent_width)
    gate_block = gate_recv.reshape(local_count, row_count).astype(jnp.float32)
    pre_act = jnp.einsum(
        "erl,elf->erf", latent_block, expert_in, preferred_element_type=jnp.float32
    )
    relu_out = jnp.maximum(pre_act, 0.0)
    back_proj = jnp.einsum(
        "erl,efl->erf", cot_block, expert_out, preferred_element_type=jnp.float32
    )
    gate_part = jnp.sum(back_proj * relu_out * relu_out, axis=2)
    scaled_act = (gate_block[:, :, None] * relu_out * relu_out).astype(jnp.bfloat16)
    pre_grad = (2.0 * gate_block[:, :, None] * relu_out * back_proj).astype(jnp.bfloat16)
    expert_out_grad = jnp.einsum(
        "erf,erl->efl", scaled_act, cot_block, preferred_element_type=jnp.float32
    )
    expert_in_grad = jnp.einsum(
        "erl,erf->elf", latent_block, pre_grad, preferred_element_type=jnp.float32
    )
    latent_back = jnp.einsum(
        "erf,elf->erl", pre_grad, expert_in, preferred_element_type=jnp.float32
    )
    latent_back = latent_back.reshape(local_count, groups, capacity, latent_width)
    gate_part = gate_part.reshape(local_count, groups, capacity)
    dispatch_full = hit_slot.astype(jnp.float32)
    dispatch_flat = dispatch_full.reshape(slot_total, tokens_here)
    rows_home, gate_home = (
        lax.all_to_all(latent_back, "expert", split_axis=1, concat_axis=1, tiled=True),
        lax.all_to_all(gate_part, "expert", split_axis=1, concat_axis=1, tiled=True),
    )
    token_sums = jnp.dot(
        dispatch_flat.T,
        rows_home.reshape(slot_total, latent_width),
        precision=lax.Precision.HIGHEST,
        preferred_element_type=jnp.float32,
    )
    by_expert = jnp.sum(dispatch_full * gate_home[:, :, :, None], axis=2)
    by_expert = by_expert.transpose(2, 1, 0).reshape(tokens_here, live_count)
    gate_local = jnp.sum(jnp.where(member, by_expert[:, None, :], 0.0), axis=2)
    latent_grad, gate_grad = lax.psum((token_sums, gate_local), "hidden")
    latent_bf = latent_grad.astype(jnp.bfloat16)
    input_grad = jnp.dot(latent_bf, down_proj, preferred_element_type=jnp.float32).astype(
        jnp.bfloat16
    )
    down_term = jnp.einsum("tl,td->ld", latent_bf, layer_input, preferred_element_type=jnp.float32)
    up_term = jnp.einsum(
        "tl,td->ld", combined_saved, output_grad, preferred_element_type=jnp.float32
    )
    down_grad, up_grad = (
        lax.psum_scatter(down_term, "expert", scatter_dimension=0, tiled=True),
        lax.psum_scatter(up_term, "expert", scatter_dimension=0, tiled=True),
    )
    return (input_grad, down_grad, up_grad, gate_grad, expert_in_grad, expert_out_grad)


def solution(mesh):
    return jax.shard_map(
        on_device,
        mesh=mesh,
        in_specs=(
            P("expert", "hidden"),
            P("expert", "hidden"),
            P("expert", None),
            P("expert", None),
            P("expert", None),
            P("expert", None),
            P(None, "hidden"),
            P(None, "hidden"),
            P("expert", None, "hidden"),
            P("expert", "hidden", None),
        ),
        out_specs=(
            P("expert", "hidden"),
            P("expert", "hidden"),
            P("expert", "hidden"),
            P("expert", None),
            P("expert", None, "hidden"),
            P("expert", "hidden", None),
        ),
        check_vma=False,
    )
```

profile of v0, /device:TPU:0, one launch (start us, length us, event | category | flops | bytes accessed | tf_op | source)
XLA Modules:
  0.0 205.3 jit_solution(8153282223888246019)
XLA Ops:
  7.2 1.1 copy-done
  8.4 2.4 %fusion.21 = f32[256,1024]{1,0:T(8,128)} fusion(bf16[256,512]{1,0:T(8,128)(2,1)} %param.11, bf16[1024,512]{1,0:T(8,128)(2,1)S(1)} %copy-done), kind=kOutput, calls=%fused_computation.44 | convolution fusion | flops 268435456 | bytes 2359296 | tf_op jit(solution)/shard_map/td,ld->tl/dot_general | solution.py:33
  10.9 1.8 fusion.22
  12.8 1.2 reduce-window.6
  14.6 1.6 convolution_convert_fusion.2
  16.2 5.2 %all-to-all-start.1 = ((bf16[1,4,24,128]{3,2,0,1:T(8,128)(2,1)}), bf16[1,4,24,128]{3,2,0,1:T(8,128)(2,1)S(1)}, u32[]{:S(2)}, u32[]{:S(2)}) async-start(bf16[1,4,24,128]{3,2,0,1:T(8,128)(2,1)} %bitcast.8), calls=%async_computation.1 | async-start | bytes 49152 | tf_op jit(solution)/shard_map/all_to_all | solution.py:69
  21.4 24.7 %reduce-scatter.4.cloned.1.call-done = f32[256,128]{1,0:T(8,128)} async-done(((f32[256,1024]{1,0:T(8,128)}), f32[256,128]{1,0:T(8,128)}) %reduce-scatter.4.cloned.1.call-update) | async-done | bytes 131088 | tf_op jit(solution)/shard_map/reduce_scatter | solution.py:49
  46.0 1.7 convolution_convert_fusion.1
  47.7 3.6 %all-to-all-start.2 = ((bf16[1,4,24,128]{3,2,0,1:T(8,128)(2,1)}), bf16[1,4,24,128]{3,2,0,1:T(8,128)(2,1)S(1)}, u32[]{:S(2)}, u32[]{:S(2)}) async-start(bf16[1,4,24,128]{3,2,0,1:T(8,128)(2,1)} %bitcast.12), calls=%async_computation.3 | async-start | bytes 49152 | tf_op jit(solution)/shard_map/all_to_all | solution.py:62
  51.3 12.9 %all_gather.6 = bf16[1,4,24,1024]{3,2,0,1:T(8,128)(2,1)S(1)} all-gather(bf16[1,4,24,128]{3,2,0,1:T(8,128)(2,1)S(1)} %all-to-all-done.1), channel_id=1, replica_groups=mesh['expert'=4,'hidden'=8] {'hidden'}, dimensions={3}, use_global_device_ids=true | all-gather | bytes 221184 | tf_op jit(solution)/shard_map/all_gather | solution.py:80
  64.2 12.9 %all_gather.7 = bf16[1,4,24,1024]{3,2,0,1:T(8,128)(2,1)S(1)} all-gather(bf16[1,4,24,128]{3,2,0,1:T(8,128)(2,1)S(1)} %all-to-all-done.2), channel_id=1, replica_groups=mesh['expert'=4,'hidden'=8] {'hidden'}, dimensions={3}, use_global_device_ids=true | all-gather | bytes 221184 | tf_op jit(solution)/shard_map/all_gather | solution.py:79
  77.5 0.4 fusion.8
  78.0 0.7 reshape.184
  78.7 4.2 %all-to-all-start.4 = ((f32[1,4,24]{2,0,1:T(1,128)}), f32[1,4,24]{2,0,1:T(1,128)S(1)}, u32[]{:S(2)}, u32[]{:S(2)}) async-start(f32[1,4,24]{2,0,1:T(1,128)} %bitcast.21), calls=%async_computation.7 | async-start | bytes 4096 | tf_op jit(solution)/shard_map/all_to_all | solution.py:111
  82.9 4.6 %all-to-all-done.4 = f32[1,4,24]{2,0,1:T(1,128)S(1)} async-done(((f32[1,4,24]{2,0,1:T(1,128)}), f32[1,4,24]{2,0,1:T(1,128)S(1)}, u32[]{:S(2)}, u32[]{:S(2)}) %all-to-all-start.4) | async-done | bytes 416 | tf_op jit(solution)/shard_map/all_to_all | solution.py:111
  87.7 7.0 %all_to_all.25 = bf16[1,4,24]{2,0,1:T(2,128)(2,1)S(1)} all-to-all(bf16[1,4,24]{2,0,1:T(2,128)(2,1)S(1)} %copy.32), channel_id=1, replica_groups=mesh['expert'=4,'hidden'=8] {'expert'}, dimensions={1} | all-to-all | bytes 384 | tf_op jit(solution)/shard_map/all_to_all | solution.py:76
  95.2 8.8 %all_to_all.26 = f32[1,4,24,1024]{3,2,0,1:T(8,128)S(1)} all-to-all(f32[1,4,24,1024]{3,2,0,1:T(8,128)S(1)} %convolution_bitcast_fusion.3), channel_id=1, replica_groups=mesh['expert'=4,'hidden'=8] {'expert'}, dimensions={1} | all-to-all | bytes 786432 | tf_op jit(solution)/shard_map/all_to_all | solution.py:110
  104.0 0.6 convolution_bitcast_fusion.2
  104.7 56.5 %all-reduce.2 = (bf16[256,1024]{1,0:T(8,128)(2,1)S(1)}, f32[256,22]{0,1:T(8,128)}) all-reduce(f32[256,1024]{1,0:T(8,128)S(1)} %convolution_bitcast_fusion.2, f32[256,22]{0,1:T(8,128)S(1)} %get-tuple-element.6), channel_id=1, replica_groups=mesh['expert'=4,'hidden'=8] {'hidden'}, use_global_device_ids=true, to_apply=%region_6.7 | all-reduce | flops 267776 | bytes 1617920 | tf_op jit(solution)/shard_map/psum | solution.py:122
  161.2 2.7 %fusion.23 = f32[1024,512]{1,0:T(8,128)} fusion(bf16[256,1024]{1,0:T(8,128)(2,1)S(1)} %get-tuple-element.8, bf16[256,512]{1,0:T(8,128)(2,1)} %param.10), kind=kOutput, calls=%fused_computation.46 | convolution fusion | flops 268435456 | bytes 2883584 | tf_op jit(solution)/shard_map/tl,td->ld/dot_general | solution.py:127
  163.9 1.5 convolution_bitcast_fusion.1
  165.4 1.5 convolution_bitcast_fusion
  166.9 1.2 convolution_convert_fusion
  168.1 30.7 %reduce-scatter.6.cloned.1.call-done = f32[256,512]{1,0:T(8,128)} async-done(((f32[1024,512]{1,0:T(8,128)}), f32[256,512]{1,0:T(8,128)}) %reduce-scatter.6.cloned.1.call-update) | async-done | bytes 524304 | tf_op jit(solution)/shard_map/reduce_scatter | solution.py:132
  (48 shorter events, 1.9 us)
Async XLA Ops:
  7.2 1.2 copy-start
  7.2 3.7 %copy-start.3 = (bf16[256,512]{1,0:T(8,128)(2,1)S(1)}, bf16[256,512]{1,0:T(8,128)(2,1)}, u32[]{:S(2)}) copy-start(bf16[256,512]{1,0:T(8,128)(2,1)} %param.11) | copy-start | bytes 786436
  7.2 3.7 %copy-start.5 = (bf16[256,1024]{1,0:T(8,128)(2,1)S(1)}, bf16[256,1024]{1,0:T(8,128)(2,1)}, u32[]{:S(2)}) copy-start(bf16[256,1024]{1,0:T(8,128)(2,1)} %param.13) | copy-start | bytes 1572868
  7.2 38.8 %reduce-scatter.4.cloned.1.call-start = ((), (), s32[]{:S(2)}) async-start(), calls=%async_computation.8 | async-start | bytes 1179648 | tf_op jit(solution)/shard_map/reduce_scatter | solution.py:49
  10.8 1.9 copy-start.6
  10.8 157.2 %reduce-scatter.8.cloned.1.call-start = ((), (), s32[]{:S(2)}) async-start(), calls=%async_computation.10 | async-start | bytes 2621440 | tf_op jit(solution)/shard_map/reduce_scatter | solution.py:133
  12.7 64.5 %copy-start.4 = (bf16[1,336,1024]{2,1,0:T(8,128)(2,1)S(1)}, bf16[1,336,1024]{2,1,0:T(8,128)(2,1)}, u32[]{:S(2)}) copy-start(bf16[1,336,1024]{2,1,0:T(8,128)(2,1)} %param.19) | copy-start | bytes 2064388
  12.7 64.8 %copy-start.1 = (bf16[1,1024,336]{1,2,0:T(8,128)(2,1)S(1)}, bf16[1,1024,336]{1,2,0:T(8,128)(2,1)}, u32[]{:S(2)}) copy-start(bf16[1,1024,336]{1,2,0:T(8,128)(2,1)} %param.18) | copy-start | bytes 2064388
  12.8 70.1 %copy-start.7 = (bf16[256,22]{0,1:T(8,128)(2,1)S(1)}, bf16[256,22]{0,1:T(8,128)(2,1)}, u32[]{:S(2)}) copy-start(bf16[256,22]{0,1:T(8,128)(2,1)} %param.15) | copy-start | bytes 33796
  16.2 31.5 %all-to-all-start.1 = ((bf16[1,4,24,128]{3,2,0,1:T(8,128)(2,1)}), bf16[1,4,24,128]{3,2,0,1:T(8,128)(2,1)S(1)}, u32[]{:S(2)}, u32[]{:S(2)}) async-start(bf16[1,4,24,128]{3,2,0,1:T(8,128)(2,1)} %bitcast.8), calls=%async_computation.1 | async-start | bytes 49152 | tf_op jit(solution)/shard_map/all_to_all | solution.py:69
  47.7 16.5 %all-to-all-start.2 = ((bf16[1,4,24,128]{3,2,0,1:T(8,128)(2,1)}), bf16[1,4,24,128]{3,2,0,1:T(8,128)(2,1)S(1)}, u32[]{:S(2)}, u32[]{:S(2)}) async-start(bf16[1,4,24,128]{3,2,0,1:T(8,128)(2,1)} %bitcast.12), calls=%async_computation.3 | async-start | bytes 49152 | tf_op jit(solution)/shard_map/all_to_all | solution.py:62
  78.7 8.8 %all-to-all-start.4 = ((f32[1,4,24]{2,0,1:T(1,128)}), f32[1,4,24]{2,0,1:T(1,128)S(1)}, u32[]{:S(2)}, u32[]{:S(2)}) async-start(f32[1,4,24]{2,0,1:T(1,128)} %bitcast.21), calls=%async_computation.7 | async-start | bytes 4096 | tf_op jit(solution)/shard_map/all_to_all | solution.py:111
  82.9 115.9 %reduce-scatter.6.cloned.1.call-start = ((), (), s32[]{:S(2)}) async-start(), calls=%async_computation.9 | async-start | bytes 2621440 | tf_op jit(solution)/shard_map/reduce_scatter | solution.py:132
  163.9 3.0 %copy-start.2 = (bf16[1024,512]{1,0:T(8,128)(2,1)S(1)}, bf16[1024,512]{1,0:T(8,128)(2,1)}, u32[]{:S(2)}) copy-start(bf16[1024,512]{1,0:T(8,128)(2,1)} %param.16) | copy-start | bytes 3145732
Sparse Core Ops, SparseCore 0:
  10.9 35.0 reduce-scatter.3
  49.6 33.3 reduce-scatter.7
  164.0 34.6 reduce-scatter.5
where the time goes:
time: 206 us; the launch traced here: 205 us
  blocking collectives  98.2 us (48%)
  waiting for transfers between devices  60 us (29%)
  matrix products  16 us (8%)
  between operations  13.9 us (7%)
  starting transfers between devices  13 us (6%)
  local copies, waits for them, and re-layouts  2.34 us (1%)
    psum x1, blocking collectives, on_device(): latent_grad, gate_grad = lax.psum((token_sums, gate_local), 'hidden')  56.5 us
    reduce_scatter x1, waiting for transfers between devices, on_device(): lax.psum_scatter(down_term, 'expert', scatter_dimension=0, tiled=True)  30.7 us
    reduce_scatter x1, waiting for transfers between devices, on_device(): lax.psum_scatter(partial_cot, 'hidden', scatter_dimension=1, tiled=True)  24.7 us
    all_gather x1, blocking collectives, on_device(): lax.all_gather(cot_piece, 'hidden', axis=3, tiled=True)  12.9 us
    all_gather x1, blocking collectives, on_device(): lax.all_gather(latent_piece, 'hidden', axis=3, tiled=True)  12.9 us
    all_to_all x1, blocking collectives, on_device(): lax.all_to_all(latent_back, 'expert', split_axis=1, concat_axis=1, tiled=...  8.82 us
    all_to_all x1, blocking collectives, on_device(): lax.all_to_all(gate_send, 'expert', split_axis=1, concat_axis=1, tiled=True)  6.99 us
    all_to_all x1, starting transfers between devices, on_device(): lax.all_to_all(latent_rows.reshape(local_count, groups, capacity, part_wi...  5.16 us
  transfers between devices with their start and end apart: 6, of which 3 were waited for; matrix products, arithmetic and copies ran while one was open for 8% of the time, Pallas kernels for 0%

commit v1 on v0

--- a/solution.py
+++ b/solution.py
@@ -1,7 +1,369 @@
+import functools
+
 import jax
 import jax.numpy as jnp
 from jax import lax
+from jax.experimental import pallas as pl
+from jax.experimental.pallas import tpu as pltpu
 from jax.sharding import PartitionSpec as P
+
+F32 = jnp.float32
+BF16 = jnp.bfloat16
+LANES = 128
+ROWS = 16
+
+
+def mm(a, b, ca, cb):
+    return lax.dot_general(a, b, (((ca,), (cb,)), ((), ())), preferred_element_type=F32)
+
+
+def rows_at(index, size):
+    return pl.ds(pl.multiple_of(index * size, size), size)
+
+
+def fused_kernel(
+    groups,
+    shares,
+    pad,
+    x_ref,
+    og_ref,
+    z_ref,
+    u_ref,
+    ids_ref,
+    gates_ref,
+    down_ref,
+    up_ref,
+    ein_ref,
+    eout_ref,
+    ig_ref,
+    dg_ref,
+    ug_ref,
+    gg_ref,
+    eig_ref,
+    eog_ref,
+    dt_s,
+    og_s,
+    og_r,
+    z_s,
+    z_r,
+    x_s,
+    x_r,
+    up_s,
+    up_r,
+    cf,
+    cs,
+    cr,
+    cag,
+    bf,
+    bs,
+    br,
+    bag,
+    home,
+    dn,
+    sems_e,
+    sems_h,
+):
+    e = lax.axis_index("expert")
+    h = lax.axis_index("hidden")
+    tokens, topk = ids_ref.shape
+    slots = groups * pad
+    latent = z_ref.shape[1]
+    block = slots // shares
+    lw = latent // groups
+
+    def expert_peer(j):
+        return lax.rem(e + j, groups)
+
+    def hidden_peer(j):
+        return lax.rem(h + j, shares)
+
+    def expert_source(j):
+        return lax.rem(e + (groups - j), groups)
+
+    def hidden_source(j):
+        return lax.rem(h + (shares - j), shares)
+
+    def to_expert(phase, j, src, dst):
+        copy = pltpu.make_async_remote_copy(
+            src_ref=src,
+            dst_ref=dst,
+            send_sem=sems_e.at[phase, 0, j],
+            recv_sem=sems_e.at[phase, 1, j],
+            device_id=(expert_peer(j), h),
+            device_id_type=pl.DeviceIdType.MESH,
+        )
+        copy.start()
+        return copy
+
+    def to_hidden(phase, j, src, dst):
+        copy = pltpu.make_async_remote_copy(
+            src_ref=src,
+            dst_ref=dst,
+            send_sem=sems_h.at[phase, 0, j],
+            recv_sem=sems_h.at[phase, 1, j],
+            device_id=(e, hidden_peer(j)),
+            device_id_type=pl.DeviceIdType.MESH,
+        )
+        copy.start()
+        return copy
+
+    barrier = pltpu.get_barrier_semaphore()
+    for j in range(1, groups):
+        pl.semaphore_signal(
+            barrier,
+            inc=1,
+            device_id=(expert_peer(j), h),
+            device_id_type=pl.DeviceIdType.MESH,
+        )
+    for j in range(1, shares):
+        pl.semaphore_signal(
+            barrier,
+            inc=1,
+            device_id=(e, hidden_peer(j)),
+            device_id_type=pl.DeviceIdType.MESH,
+        )
+
+    ids = ids_ref[...]
+    gates = gates_ref[...].astype(F32)
+    lane = lax.broadcasted_iota(jnp.int32, (tokens, slots), 1)
+    lane_expert = lane // pad
+    member = jnp.zeros((tokens, slots), F32)
+    gate_token = jnp.zeros((tokens, slots), F32)
+    for k in range(topk):
+        hit = ids[:, k : k + 1] == lane_expert
+        member = jnp.where(hit, 1.0, member)
+        gate_token = jnp.where(hit, gates[:, k : k + 1], gate_token)
+    row_t = lax.broadcasted_iota(jnp.int32, (tokens, tokens), 0)
+    col_t = lax.broadcasted_iota(jnp.int32, (tokens, tokens), 1)
+    earlier = jnp.where(col_t < row_t, 1.0, 0.0).astype(BF16)
+    before = mm(earlier, member.astype(BF16), 1, 0)
+    rank = (lane - lane_expert * pad).astype(F32)
+    disp_t = jnp.where(before == rank, member, 0.0)
+    disp = disp_t.T.astype(BF16)
+    dt_s[...] = disp_t.astype(BF16)
+
+    og_s[...] = mm(disp, og_ref[...], 1, 0).astype(BF16).reshape(og_s.shape)
+    pl.semaphore_wait(barrier, groups + shares - 2)
+    og_c = [
+        to_expert(0, j, og_s.at[expert_peer(j)], og_r.at[e]) for j in range(1, groups)
+    ]
+    z_s[:, :, 0:latent] = mm(disp, z_ref[...], 1, 0).astype(BF16).reshape(groups, pad, latent)
+    gate_all = mm(disp, gate_token.astype(BF16), 1, 0)
+    srow = lax.broadcasted_iota(jnp.int32, (slots, slots), 0)
+    scol = lax.broadcasted_iota(jnp.int32, (slots, slots), 1)
+    gate_col = jnp.sum(
+        jnp.where(scol == (srow // pad) * pad, gate_all, 0.0), axis=1, keepdims=True
+    )
+    z_s[:, :, latent : latent + LANES] = (
+        jnp.broadcast_to(gate_col, (slots, LANES)).astype(BF16).reshape(groups, pad, LANES)
+    )
+    z_c = [to_expert(1, j, z_s.at[expert_peer(j)], z_r.at[e]) for j in range(1, groups)]
+    og_r[e] = og_s[e]
+    z_r[e] = z_s[e]
+    x_s[...] = mm(disp, x_ref[...], 1, 0).astype(BF16).reshape(x_s.shape)
+    x_r[:, rows_at(e, pad), :] = x_s[...]
+    for j in range(1, groups):
+        up_s[j - 1] = mm(
+            u_ref[:, rows_at(expert_peer(j), lw)], og_ref[...], 0, 0
+        ).astype(BF16)
+    ug_ref[...] = mm(u_ref[:, rows_at(e, lw)], og_ref[...], 0, 0)
+
+    for c in og_c:
+        c.wait_recv()
+    cot_part = mm(og_r[...].reshape(slots, og_ref.shape[1]), up_ref[...], 1, 1)
+    cs[...] = cot_part.astype(BF16)
+    cf[...] = cot_part
+    crs = [
+        to_hidden(0, j, cs.at[rows_at(hidden_peer(j), block)], cr.at[h])
+        for j in range(1, shares)
+    ]
+    for c in z_c:
+        c.wait_recv()
+    x_c = [
+        to_expert(2, j, x_s, x_r.at[:, rows_at(e, pad), :]) for j in range(1, groups)
+    ]
+    up_c = [to_expert(3, j, up_s.at[j - 1], up_r.at[j - 1]) for j in range(1, groups)]
+    zb = z_r[:, :, 0:latent].reshape(slots, latent)
+    gate_b = z_r[:, :, latent : latent + LANES].astype(F32).reshape(slots, LANES)[:, 0:1]
+    act = jnp.maximum(mm(zb, ein_ref[...], 1, 0), 0.0)
+    square = act * act
+    scaled = (gate_b * square).astype(BF16)
+    cot = cf[rows_at(h, block), :]
+    for j in range(1, shares):
+        crs[j - 1].wait_recv()
+        cot = cot + cr[hidden_source(j)].astype(F32)
+    cag[rows_at(h, block), :] = cot.astype(BF16)
+    cagc = [
+        to_hidden(1, j, cag.at[rows_at(h, block)], cag.at[rows_at(h, block)])
+        for j in range(1, shares)
+    ]
+    for c in cagc:
+        c.wait_recv()
+
+    cotb = cag[...]
+    back = mm(cotb, eout_ref[...], 1, 1)
+    gate_part = jnp.sum(back * square, axis=1, keepdims=True)
+    pre_grad = ((2.0 * gate_b) * act * back).astype(BF16)
+    part = mm(pre_grad, ein_ref[...], 1, 1)
+    gate_wide = jnp.broadcast_to(gate_part, (slots, LANES))
+    bf[:, 0:latent] = part
+    bf[:, latent : latent + LANES] = gate_wide
+    bs[:, 0:latent] = part.astype(BF16)
+    bs[:, latent : latent + LANES] = gate_wide.astype(BF16)
+    brs = [
+        to_hidden(2, j, bs.at[rows_at(hidden_peer(j), block)], br.at[h])
+        for j in range(1, shares)
+    ]
+    eog_ref[0] = mm(scaled, cotb, 0, 0)
+    eig_ref[0] = mm(zb, pre_grad, 0, 0)
+    total = bf[rows_at(h, block), :]
+    for j in range(1, shares):
+        brs[j - 1].wait_recv()
+        total = total + br[hidden_source(j)].astype(F32)
+    bag[rows_at(h, block), :] = total.astype(BF16)
+    bagc = [
+        to_hidden(3, j, bag.at[rows_at(h, block)], bag.at[rows_at(h, block)])
+        for j in range(1, shares)
+    ]
+    for j in range(1, groups):
+        up_c[j - 1].wait_recv()
+        ug_ref[...] += up_r[j - 1].astype(F32)
+    for c in x_c:
+        c.wait_recv()
+    for c in bagc:
+        c.wait_recv()
+
+    home_c = [
+        to_expert(4, j, bag.at[rows_at(expert_peer(j), pad)], home.at[rows_at(e, pad)])
+        for j in range(1, groups)
+    ]
+    dn_c = [
+        to_expert(5, j, bag.at[:, rows_at(expert_peer(j), lw)], dn.at[e])
+        for j in range(1, groups)
+    ]
+    home[rows_at(e, pad), :] = bag[rows_at(e, pad), :]
+    dn[e] = bag[:, rows_at(e, lw)]
+    for c in home_c:
+        c.wait_recv()
+    disp_home = dt_s[...]
+    latent_grad = mm(disp_home, home[:, 0:latent], 1, 0).astype(BF16)
+    ig_ref[...] = mm(latent_grad, down_ref[...], 1, 0).astype(BF16)
+    gate_rows = home[:, latent : latent + LANES].astype(F32)
+    wrow = lax.broadcasted_iota(jnp.int32, (slots, LANES), 0)
+    wcol = lax.broadcasted_iota(jnp.int32, (slots, LANES), 1)
+    gate_mat = jnp.where(wcol == wrow // pad, gate_rows, 0.0).astype(BF16)
+    gate_by = mm(disp_home, gate_mat, 1, 0)
+    gate_out = jnp.zeros((tokens, topk), F32)
+    for n in range(groups):
+        gate_out = jnp.where(ids == n, gate_by[:, n : n + 1], gate_out)
+    gg_ref[...] = gate_out
+    for c in dn_c:
+        c.wait_recv()
+    dg_ref[...] = mm(
+        dn[...].reshape(groups * slots, lw),
+        x_r[...].reshape(groups * slots, x_ref.shape[1]),
+        0,
+        0,
+    )
+    for c in og_c + z_c + crs + x_c + up_c + cagc + brs + bagc + home_c + dn_c:
+        c.wait_send()
+
+
+def fused(
+    layer_input,
+    output_grad,
+    latent_saved,
+    combined_saved,
+    expert_ids,
+    gate_values,
+    down_proj,
+    up_proj,
+    expert_in,
+    expert_out,
+):
+    groups = lax.axis_size("expert")
+    shares = lax.axis_size("hidden")
+    tokens, width = layer_input.shape
+    latent = latent_saved.shape[1]
+    ff = expert_in.shape[2]
+    pad = padded_rows(tokens)
+    slots = groups * pad
+    block = slots // shares
+    wide = latent + LANES
+    lw = latent // groups
+    vmem = pl.BlockSpec(memory_space=pltpu.VMEM)
+    return pl.pallas_call(
+        functools.partial(fused_kernel, groups, shares, pad),
+        out_shape=(
+            jax.ShapeDtypeStruct((tokens, width), BF16),
+            jax.ShapeDtypeStruct((lw, width), F32),
+            jax.ShapeDtypeStruct((lw, width), F32),
+            jax.ShapeDtypeStruct(expert_ids.shape, F32),
+            jax.ShapeDtypeStruct(expert_in.shape, F32),
+            jax.ShapeDtypeStruct(expert_out.shape, F32),
+        ),
+        in_specs=[vmem] * 10,
+        out_specs=[vmem] * 6,
+        scratch_shapes=[
+            pltpu.VMEM((tokens, slots), BF16),
+            pltpu.VMEM((groups, pad, width), BF16),
+            pltpu.VMEM((groups, pad, width), BF16),
+            pltpu.VMEM((groups, pad, wide), BF16),
+            pltpu.VMEM((groups, pad, wide), BF16),
+            pltpu.VMEM((groups, pad, width), BF16),
+            pltpu.VMEM((groups, slots, width), BF16),
+            pltpu.VMEM((groups - 1, lw, width), BF16),
+            pltpu.VMEM((groups - 1, lw, width), BF16),
+            pltpu.VMEM((slots, latent), F32),
+            pltpu.VMEM((slots, latent), BF16),
+            pltpu.VMEM((shares, block, latent), BF16),
+            pltpu.VMEM((slots, latent), BF16),
+            pltpu.VMEM((slots, wide), F32),
+            pltpu.VMEM((slots, wide), BF16),
+            pltpu.VMEM((shares, block, wide), BF16),
+            pltpu.VMEM((slots, wide), BF16),
+            pltpu.VMEM((slots, wide), BF16),
+            pltpu.VMEM((groups, slots, lw), BF16),
+            pltpu.SemaphoreType.DMA((6, 2, groups)),
+            pltpu.SemaphoreType.DMA((4, 2, shares)),
+        ],
+        compiler_params=pltpu.CompilerParams(
+            collective_id=0, has_side_effects=True, vmem_limit_bytes=48 * 1024 * 1024
+        ),
+    )(
+        layer_input,
+        output_grad,
+        latent_saved,
+        combined_saved,
+        expert_ids,
+        gate_values,
+        down_proj,
+        up_proj,
+        expert_in[0],
+        expert_out[0],
+    )
+
+
+def padded_rows(tokens):
+    return -(-(tokens * 3 // 32) // ROWS) * ROWS
+
+
+def fits(layer_input, latent_saved, expert_in):
+    groups = lax.axis_size("expert")
+    shares = lax.axis_size("hidden")
+    slots = groups * padded_rows(layer_input.shape[0])
+    return (
+        expert_in.shape[0] == 1
+        and slots % (ROWS * shares) == 0
+        and slots % LANES == 0
+        and latent_saved.shape[1] % (LANES * groups) == 0
+        and layer_input.shape[1] % LANES == 0
+    )
+
+
+def per_device(*arrays):
+    run = fused if fits(arrays[0], arrays[2], arrays[8]) else on_device
+    return run(*arrays)
 
 
 def slot_layout(table, groups, local_count):
@@ -33,7 +395,11 @@
     partial_cot = jnp.einsum("td,ld->tl", output_grad, up_proj, preferred_element_type=jnp.float32)
     member = expert_ids[:, :, None] == jnp.arange(live_count, dtype=jnp.int32)[None, None, :]
     per_token = jnp.sum(member.astype(jnp.int32), axis=1)
-    before = jnp.cumsum(per_token, axis=0) - per_token
+    token_iota = jnp.arange(tokens_here, dtype=jnp.int32)
+    earlier = (token_iota[None, :] < token_iota[:, None]).astype(jnp.bfloat16)
+    before = jnp.dot(
+        earlier, per_token.astype(jnp.bfloat16), preferred_element_type=jnp.float32
+    ).astype(jnp.int32)
     gate_token = jnp.sum(
         jnp.where(member, gate_values.astype(jnp.float32)[:, :, None], 0.0), axis=1
     )
@@ -137,7 +503,7 @@
 
 def solution(mesh):
     return jax.shard_map(
-        on_device,
+        per_device,
         mesh=mesh,
         in_specs=(
             P("expert", "hidden"),

time: 206 us -> 69.3 us (0.34)
  blocking collectives: 98.2 us -> 0 us
  waiting for transfers between devices: 60 us -> 0 us
  Pallas kernels: 0 us -> 50 us
  matrix products: 16 us -> 0 us
  local copies, waits for them, and re-layouts: 2.34 us -> 18.1 us
  between operations: 13.9 us -> 0.71 us
  starting transfers between devices: 13 us -> 0 us
    psum x1 -> x0, blocking collectives: 56.5 us -> none  [on_device(): latent_grad, gate_grad = lax.psum((token_sums, gate_local), 'hidden')]
    reduce_scatter x3 -> x0, waiting for transfers between devices: 55.4 us -> none  [the longest x1 30.7 us: on_device(): lax.psum_scatter(down_term, 'expert', scatter_dimension=0, tiled=True)]
    pallas_call x0 -> x1, Pallas kernels: none -> 50 us  [fused(): pl.pallas_call(functools.partial(fused_kernel, groups, shares, pad), out_...]
    all_gather x2 -> x0, blocking collectives: 25.9 us -> none  [the longest x1 12.9 us: on_device(): lax.all_gather(cot_piece, 'hidden', axis=3, tiled=True)]
    dot_general x12 -> x0, matrix products: 16 us -> none  [the longest x1 2.72 us: on_device(): jnp.einsum('tl,td->ld', latent_bf, layer_input, preferred_element_type=jn...]
    all_to_all x2 -> x0, blocking collectives: 15.8 us -> none  [the longest x1 8.82 us: on_device(): lax.all_to_all(latent_back, 'expert', split_axis=1, concat_axis=1, tiled=...]
    all_to_all x3 -> x0, starting transfers between devices: 12.9 us -> none  [the longest x1 5.16 us: on_device(): lax.all_to_all(latent_rows.reshape(local_count, groups, capacity, part_wi...]
    unnamed x16 -> x29, local copies, waits for them, and re-layouts: 1.19 us -> 13.5 us
  transfers between devices with their start and end apart: 6 -> 0, of which waited for: 3 -> 0; matrix products, arithmetic and copies ran while one was open for 8% -> 0% of each run, Pallas kernels for 0% -> 0%
where the time goes in v1:
time: 69.3 us; the launch traced here: 68.8 us
  Pallas kernels  50 us (72%)
  local copies, waits for them, and re-layouts  18.1 us (26%)
  between operations  0.71 us (1%)
    pallas_call x1, Pallas kernels, fused(): pl.pallas_call(functools.partial(fused_kernel, groups, shares, pad), out_...  50 us
    unnamed x29, local copies, waits for them, and re-layouts  13.5 us
    pallas_call x2, local copies, waits for them, and re-layouts, fused(): pl.pallas_call(functools.partial(fused_kernel, groups, shares, pad), out_...  4.58 us

profile of v1, /device:TPU:0, one launch (start us, length us, event | category | flops | bytes accessed | tf_op | source)
XLA Modules:
  0.0 68.8 jit_solution(7300818075104621028)
XLA Ops:
  0.6 0.0 copy-start
  0.6 0.0 copy-start.2
  0.7 1.6 %copy.18.gates_ref = bf16[256,22]{1,0:T(8,128)(2,1)} copy(bf16[256,22]{0,1:T(8,128)(2,1)} %param.15) | data formatting | bytes 22528 | tf_op args[5]
  2.2 0.8 %copy.17.ids_ref = s32[256,22]{1,0:T(8,128)S(1)} copy(s32[256,22]{0,1:T(8,128)} %param.14) | data formatting | bytes 45056 | tf_op args[4]
  3.1 1.4 %copy.16 = bf16[1,1024,336]{2,1,0:T(8,128)(2,1)S(1)} copy(bf16[1,1024,336]{1,2,0:T(8,128)(2,1)} %param.18) | data formatting | bytes 1376256 | tf_op args[8]
  4.5 0.0 copy-done
  4.5 0.0 copy-done.2
  4.5 0.0 copy-start.1
  4.6 1.1 %copy-done.1 = bf16[1,336,1024]{2,1,0:T(8,128)(2,1)S(1)} copy-done((bf16[1,336,1024]{2,1,0:T(8,128)(2,1)S(1)}, bf16[1,336,1024]{2,1,0:T(8,128)(2,1)}, u32[]{:S(2)}) %copy-start.1) | copy-done | bytes 688152
  5.6 1.0 %copy-done.3 = bf16[256,1024]{1,0:T(8,128)(2,1)S(1)} copy-done((bf16[256,1024]{1,0:T(8,128)(2,1)S(1)}, bf16[256,1024]{1,0:T(8,128)(2,1)}, u32[]{:S(2)}) %copy-start.3) | copy-done | bytes 524312
  6.7 0.9 %copy-done.6 = bf16[256,512]{1,0:T(8,128)(2,1)S(1)} copy-done((bf16[256,512]{1,0:T(8,128)(2,1)S(1)}, bf16[256,512]{1,0:T(8,128)(2,1)}, u32[]{:S(2)}) %copy-start.6) | copy-done | bytes 262168
  7.6 0.9 %copy-done.7 = bf16[256,512]{1,0:T(8,128)(2,1)S(1)} copy-done((bf16[256,512]{1,0:T(8,128)(2,1)S(1)}, bf16[256,512]{1,0:T(8,128)(2,1)}, u32[]{:S(2)}) %copy-start.7) | copy-done | bytes 262168
  8.6 0.8 %copy-done.8 = bf16[256,22]{1,0:T(8,128)(2,1)S(1)} copy-done((bf16[256,22]{1,0:T(8,128)(2,1)S(1)}, bf16[256,22]{1,0:T(8,128)(2,1)}, u32[]{:S(2)}) %copy-start.8) | copy-done | bytes 11288
  9.4 50.0 %shard_map.145 = (bf16[256,512]{1,0:T(8,128)(2,1)S(1)}, f32[256,512]{1,0:T(8,128)S(1)}, f32[256,512]{1,0:T(8,128)S(1)}, f32[256,22]{1,0:T(8,128)S(1)}, f32[1,1024,336]{2,1,0:T(8,128)}, /*index=5*/f32[1,336,1024]{2,1,0:T(8,128)}) custom-call(bf16[256,512]{1,0:T(8,128)(2,1)S(1)} %copy-done.6, bf16[256,512]{1,0:T(8,128)(2,1)S(1)} %copy-done.7, ...), custom_call_target="tpu_custom_call" | custom-call | tf_op jit(solution)/shard_map/pallas_call | solution.py:295
  59.5 0.0 copy-start.4
  59.5 0.7 %copy-done.4 = bf16[256,512]{1,0:T(8,128)(2,1)} copy-done((bf16[256,512]{1,0:T(8,128)(2,1)}, bf16[256,512]{1,0:T(8,128)(2,1)S(1)}, u32[]{:S(2)}) %copy-start.4) | copy-done | bytes 262168
  60.2 0.7 copy-done.9
  60.8 1.6 %copy.19 = f32[256,22]{0,1:T(8,128)} copy(f32[256,22]{1,0:T(8,128)} %copy-done.9) | data formatting | bytes 45056 | tf_op jit(solution)/shard_map/pallas_call | solution.py:295
  62.4 3.0 %copy.20 = f32[1,1024,336]{1,2,0:T(8,128)} copy(f32[1,1024,336]{2,1,0:T(8,128)} %get-tuple-element.10) | data formatting | bytes 2752512 | tf_op jit(solution)/shard_map/pallas_call | solution.py:295
  65.4 0.0 copy-done.5
  65.4 0.7 %copy.25 = bf16[256,512]{1,0:T(8,128)(2,1)} copy(bf16[256,512]{1,0:T(8,128)(2,1)S(1)} %copy-done.5) | data formatting | bytes 524288
  66.1 0.8 %copy.26 = f32[256,512]{1,0:T(8,128)} copy(f32[256,512]{1,0:T(8,128)S(1)} %get-tuple-element.19) | data formatting | bytes 1048576
  66.9 0.8 %copy.27 = f32[256,512]{1,0:T(8,128)} copy(f32[256,512]{1,0:T(8,128)S(1)} %get-tuple-element.20) | data formatting | bytes 1048576
  67.7 1.1 %copy.28 = f32[1,336,1024]{2,1,0:T(8,128)} copy(f32[1,336,1024]{2,1,0:T(8,128)S(1)} %copy-done.10) | data formatting | bytes 2752512
  (8 shorter events, 0.0 us)
Async XLA Ops:
  0.6 3.9 %copy-start = (bf16[1024,512]{1,0:T(8,128)(2,1)S(1)}, bf16[1024,512]{1,0:T(8,128)(2,1)}, u32[]{:S(2)}) copy-start(bf16[1024,512]{1,0:T(8,128)(2,1)} %down_ref.1) | copy-start | bytes 3145732
  0.6 3.9 %copy-start.2 = (bf16[256,1024]{1,0:T(8,128)(2,1)S(1)}, bf16[256,1024]{1,0:T(8,128)(2,1)}, u32[]{:S(2)}) copy-start(bf16[256,1024]{1,0:T(8,128)(2,1)} %z_ref.1) | copy-start | bytes 1572868
  4.5 1.1 %copy-start.1 = (bf16[1,336,1024]{2,1,0:T(8,128)(2,1)S(1)}, bf16[1,336,1024]{2,1,0:T(8,128)(2,1)}, u32[]{:S(2)}) copy-start(bf16[1,336,1024]{2,1,0:T(8,128)(2,1)} %param.19) | copy-start | bytes 2064388
  5.6 1.0 %copy-start.3 = (bf16[256,1024]{1,0:T(8,128)(2,1)S(1)}, bf16[256,1024]{1,0:T(8,128)(2,1)}, u32[]{:S(2)}) copy-start(bf16[256,1024]{1,0:T(8,128)(2,1)} %u_ref.1) | copy-start | bytes 1572868
  6.7 0.9 %copy-start.6 = (bf16[256,512]{1,0:T(8,128)(2,1)S(1)}, bf16[256,512]{1,0:T(8,128)(2,1)}, u32[]{:S(2)}) copy-start(bf16[256,512]{1,0:T(8,128)(2,1)} %x_ref.1) | copy-start | bytes 786436
  7.6 0.9 %copy-start.7 = (bf16[256,512]{1,0:T(8,128)(2,1)S(1)}, bf16[256,512]{1,0:T(8,128)(2,1)}, u32[]{:S(2)}) copy-start(bf16[256,512]{1,0:T(8,128)(2,1)} %og_ref.1) | copy-start | bytes 786436
  8.6 0.8 %copy-start.8 = (bf16[256,22]{1,0:T(8,128)(2,1)S(1)}, bf16[256,22]{1,0:T(8,128)(2,1)}, u32[]{:S(2)}) copy-start(bf16[256,22]{1,0:T(8,128)(2,1)} %copy.18.gates_ref) | copy-start | bytes 33796
  59.5 0.7 %copy-start.4 = (bf16[256,512]{1,0:T(8,128)(2,1)}, bf16[256,512]{1,0:T(8,128)(2,1)S(1)}, u32[]{:S(2)}) copy-start(bf16[256,512]{1,0:T(8,128)(2,1)S(1)} %get-tuple-element.18) | copy-start | bytes 786436
  60.2 0.7 copy-start.9
  62.4 3.0 %copy-start.5 = (bf16[256,512]{1,0:T(8,128)(2,1)S(1)}, bf16[256,512]{1,0:T(8,128)(2,1)}, u32[]{:S(2)}) copy-start(bf16[256,512]{1,0:T(8,128)(2,1)} %copy-done.4) | copy-start | bytes 786436
  65.4 2.3 %copy-start.10 = (f32[1,336,1024]{2,1,0:T(8,128)S(1)}, f32[1,336,1024]{2,1,0:T(8,128)}, u32[]{:S(2)}) copy-start(f32[1,336,1024]{2,1,0:T(8,128)} %get-tuple-element.23) | copy-start | bytes 4128772

commit v2 on v1

--- a/solution.py
+++ b/solution.py
@@ -25,47 +25,54 @@
     groups,
     shares,
     pad,
+    x_hbm,
+    og_hbm,
+    z_hbm,
+    u_hbm,
+    ids_hbm,
+    gates_hbm,
+    up_hbm,
+    ein_hbm,
+    eout_hbm,
+    disp_ref,
+    scaled_ref,
+    pre_ref,
+    zb_ref,
+    cag,
+    home,
+    dn,
+    x_r,
+    ug_ref,
     x_ref,
     og_ref,
     z_ref,
     u_ref,
     ids_ref,
     gates_ref,
-    down_ref,
     up_ref,
     ein_ref,
     eout_ref,
-    ig_ref,
-    dg_ref,
-    ug_ref,
-    gg_ref,
-    eig_ref,
-    eog_ref,
-    dt_s,
     og_s,
     og_r,
     z_s,
     z_r,
     x_s,
-    x_r,
     up_s,
     up_r,
     cf,
     cs,
     cr,
-    cag,
     bf,
     bs,
     br,
     bag,
-    home,
-    dn,
+    sems_in,
     sems_e,
     sems_h,
 ):
     e = lax.axis_index("expert")
     h = lax.axis_index("hidden")
-    tokens, topk = ids_ref.shape
+    tokens = ids_ref.shape[1]
     slots = groups * pad
     latent = z_ref.shape[1]
     block = slots // shares
@@ -106,6 +113,16 @@
         )
         copy.start()
         return copy
+
+    sources = (ids_hbm, gates_hbm, og_hbm, z_hbm, up_hbm, ein_hbm, x_hbm, u_hbm, eout_hbm)
+    targets = (ids_ref, gates_ref, og_ref, z_ref, up_ref, ein_ref, x_ref, u_ref, eout_ref)
+    loads = [
+        pltpu.make_async_copy(src, dst, sems_in.at[n])
+        for n, (src, dst) in enumerate(zip(sources, targets))
+    ]
+    for load in loads:
+        load.start()
+    ids_in, gates_in, og_in, z_in, up_in, ein_in, x_in, u_in, eout_in = loads
 
     barrier = pltpu.get_barrier_semaphore()
     for j in range(1, groups):
@@ -123,45 +140,51 @@
             device_id_type=pl.DeviceIdType.MESH,
         )
 
+    row_t = lax.broadcasted_iota(jnp.int32, (tokens, tokens), 0)
+    col_t = lax.broadcasted_iota(jnp.int32, (tokens, tokens), 1)
+    earlier = jnp.where(row_t < col_t, 1.0, 0.0).astype(BF16)
+    ids_in.wait()
+    gates_in.wait()
     ids = ids_ref[...]
     gates = gates_ref[...].astype(F32)
-    lane = lax.broadcasted_iota(jnp.int32, (tokens, slots), 1)
-    lane_expert = lane // pad
-    member = jnp.zeros((tokens, slots), F32)
-    gate_token = jnp.zeros((tokens, slots), F32)
-    for k in range(topk):
-        hit = ids[:, k : k + 1] == lane_expert
-        member = jnp.where(hit, 1.0, member)
-        gate_token = jnp.where(hit, gates[:, k : k + 1], gate_token)
-    row_t = lax.broadcasted_iota(jnp.int32, (tokens, tokens), 0)
-    col_t = lax.broadcasted_iota(jnp.int32, (tokens, tokens), 1)
-    earlier = jnp.where(col_t < row_t, 1.0, 0.0).astype(BF16)
-    before = mm(earlier, member.astype(BF16), 1, 0)
-    rank = (lane - lane_expert * pad).astype(F32)
-    disp_t = jnp.where(before == rank, member, 0.0)
-    disp = disp_t.T.astype(BF16)
-    dt_s[...] = disp_t.astype(BF16)
+    member_rows = []
+    gate_rows = []
+    for n in range(groups):
+        hit = ids == n
+        member_rows.append(jnp.sum(jnp.where(hit, 1.0, 0.0), axis=0, keepdims=True))
+        gate_rows.append(jnp.sum(jnp.where(hit, gates, 0.0), axis=0, keepdims=True))
+    member = jnp.concatenate(
+        [jnp.broadcast_to(row, (pad, tokens)) for row in member_rows], axis=0
+    )
+    gate_token = jnp.concatenate(
+        [jnp.broadcast_to(row, (pad, tokens)) for row in gate_rows], axis=0
+    )
+    before = mm(member.astype(BF16), earlier, 1, 0)
+    slot = lax.broadcasted_iota(jnp.int32, (slots, tokens), 0)
+    rank = lax.rem(slot, pad).astype(F32)
+    chosen = jnp.where(before == rank, member, 0.0)
+    disp = chosen.astype(BF16)
+    disp_ref[...] = disp
+    og_in.wait()
 
     og_s[...] = mm(disp, og_ref[...], 1, 0).astype(BF16).reshape(og_s.shape)
     pl.semaphore_wait(barrier, groups + shares - 2)
     og_c = [
         to_expert(0, j, og_s.at[expert_peer(j)], og_r.at[e]) for j in range(1, groups)
     ]
+    z_in.wait()
     z_s[:, :, 0:latent] = mm(disp, z_ref[...], 1, 0).astype(BF16).reshape(groups, pad, latent)
-    gate_all = mm(disp, gate_token.astype(BF16), 1, 0)
-    srow = lax.broadcasted_iota(jnp.int32, (slots, slots), 0)
-    scol = lax.broadcasted_iota(jnp.int32, (slots, slots), 1)
-    gate_col = jnp.sum(
-        jnp.where(scol == (srow // pad) * pad, gate_all, 0.0), axis=1, keepdims=True
-    )
+    gate_col = jnp.sum(chosen * gate_token, axis=1, keepdims=True)
     z_s[:, :, latent : latent + LANES] = (
         jnp.broadcast_to(gate_col, (slots, LANES)).astype(BF16).reshape(groups, pad, LANES)
     )
     z_c = [to_expert(1, j, z_s.at[expert_peer(j)], z_r.at[e]) for j in range(1, groups)]
     og_r[e] = og_s[e]
     z_r[e] = z_s[e]
+    x_in.wait()
     x_s[...] = mm(disp, x_ref[...], 1, 0).astype(BF16).reshape(x_s.shape)
     x_r[:, rows_at(e, pad), :] = x_s[...]
+    u_in.wait()
     for j in range(1, groups):
         up_s[j - 1] = mm(
             u_ref[:, rows_at(expert_peer(j), lw)], og_ref[...], 0, 0
@@ -170,6 +193,7 @@
 
     for c in og_c:
         c.wait_recv()
+    up_in.wait()
     cot_part = mm(og_r[...].reshape(slots, og_ref.shape[1]), up_ref[...], 1, 1)
     cs[...] = cot_part.astype(BF16)
     cf[...] = cot_part
@@ -185,9 +209,12 @@
     up_c = [to_expert(3, j, up_s.at[j - 1], up_r.at[j - 1]) for j in range(1, groups)]
     zb = z_r[:, :, 0:latent].reshape(slots, latent)
     gate_b = z_r[:, :, latent : latent + LANES].astype(F32).reshape(slots, LANES)[:, 0:1]
-    act = jnp.maximum(mm(zb, ein_ref[...], 1, 0), 0.0)
+    zb_ref[...] = zb
+    ein_in.wait()
+    act = jnp.maximum(mm(zb, ein_ref[...], 1, 1), 0.0)
     square = act * act
-    scaled = (gate_b * square).astype(BF16)
+    scaled_ref[...] = (gate_b * square).astype(BF16)
+    eout_in.wait()
     cot = cf[rows_at(h, block), :]
     for j in range(1, shares):
         crs[j - 1].wait_recv()
@@ -204,7 +231,8 @@
     back = mm(cotb, eout_ref[...], 1, 1)
     gate_part = jnp.sum(back * square, axis=1, keepdims=True)
     pre_grad = ((2.0 * gate_b) * act * back).astype(BF16)
-    part = mm(pre_grad, ein_ref[...], 1, 1)
+    pre_ref[...] = pre_grad
+    part = mm(pre_grad, ein_ref[...], 1, 0)
     gate_wide = jnp.broadcast_to(gate_part, (slots, LANES))
     bf[:, 0:latent] = part
     bf[:, latent : latent + LANES] = gate_wide
@@ -214,8 +242,6 @@
         to_hidden(2, j, bs.at[rows_at(hidden_peer(j), block)], br.at[h])
         for j in range(1, shares)
     ]
-    eog_ref[0] = mm(scaled, cotb, 0, 0)
-    eig_ref[0] = mm(zb, pre_grad, 0, 0)
     total = bf[rows_at(h, block), :]
     for j in range(1, shares):
         brs[j - 1].wait_recv()
@@ -243,30 +269,74 @@
     ]
     home[rows_at(e, pad), :] = bag[rows_at(e, pad), :]
     dn[e] = bag[:, rows_at(e, lw)]
-    for c in home_c:
+    for c in home_c + dn_c:
         c.wait_recv()
-    disp_home = dt_s[...]
-    latent_grad = mm(disp_home, home[:, 0:latent], 1, 0).astype(BF16)
-    ig_ref[...] = mm(latent_grad, down_ref[...], 1, 0).astype(BF16)
-    gate_rows = home[:, latent : latent + LANES].astype(F32)
-    wrow = lax.broadcasted_iota(jnp.int32, (slots, LANES), 0)
-    wcol = lax.broadcasted_iota(jnp.int32, (slots, LANES), 1)
-    gate_mat = jnp.where(wcol == wrow // pad, gate_rows, 0.0).astype(BF16)
-    gate_by = mm(disp_home, gate_mat, 1, 0)
-    gate_out = jnp.zeros((tokens, topk), F32)
-    for n in range(groups):
-        gate_out = jnp.where(ids == n, gate_by[:, n : n + 1], gate_out)
-    gg_ref[...] = gate_out
-    for c in dn_c:
-        c.wait_recv()
-    dg_ref[...] = mm(
-        dn[...].reshape(groups * slots, lw),
-        x_r[...].reshape(groups * slots, x_ref.shape[1]),
+    for c in og_c + z_c + crs + x_c + up_c + cagc + brs + bagc + home_c + dn_c:
+        c.wait_send()
+
+
+def outputs_kernel(
+    groups,
+    pad,
+    disp_ref,
+    scaled_ref,
+    pre_ref,
+    zb_ref,
+    cot_ref,
+    home_ref,
+    dn_ref,
+    x_ref,
+    ug_ref,
+    ids_ref,
+    down_ref,
+    ig_hbm,
+    dg_hbm,
+    ug_hbm,
+    gg_hbm,
+    eig_hbm,
+    eog_hbm,
+    ig_v,
+    dg_v,
+    gg_v,
+    eig_v,
+    eog_v,
+    sems,
+):
+    slots = groups * pad
+    latent = cot_ref.shape[1]
+    stores = []
+
+    def store(src, dst):
+        copy = pltpu.make_async_copy(src, dst, sems.at[len(stores)])
+        copy.start()
+        stores.append(copy)
+
+    store(ug_ref, ug_hbm)
+    eog_v[...] = mm(scaled_ref[...], cot_ref[...], 0, 0)
+    store(eog_v, eog_hbm)
+    eig_v[...] = mm(pre_ref[...], zb_ref[...], 0, 0)
+    store(eig_v, eig_hbm)
+    dg_v[...] = mm(
+        dn_ref[...].reshape(groups * slots, dn_ref.shape[2]),
+        x_ref[...].reshape(groups * slots, x_ref.shape[2]),
         0,
         0,
     )
-    for c in og_c + z_c + crs + x_c + up_c + cagc + brs + bagc + home_c + dn_c:
-        c.wait_send()
+    store(dg_v, dg_hbm)
+    disp = disp_ref[...]
+    latent_grad = mm(disp, home_ref[:, 0:latent], 0, 0).astype(BF16)
+    ig_v[...] = mm(latent_grad, down_ref[...], 1, 0).astype(BF16)
+    store(ig_v, ig_hbm)
+    by_slot = home_ref[:, latent : latent + LANES].astype(F32)[:, 0:1] * disp.astype(F32)
+    ids = ids_ref[...]
+    gate_out = jnp.zeros(ids.shape, F32)
+    for n in range(groups):
+        by_token = jnp.sum(by_slot[n * pad : (n + 1) * pad], axis=0, keepdims=True)
+        gate_out = jnp.where(ids == n, by_token, gate_out)
+    gg_v[...] = gate_out
+    store(gg_v, gg_hbm)
+    for copy in stores:
+        copy.wait()
 
 
 def fused(
@@ -292,56 +362,78 @@
     wide = latent + LANES
     lw = latent // groups
     vmem = pl.BlockSpec(memory_space=pltpu.VMEM)
-    return pl.pallas_call(
+    hbm = pl.BlockSpec(memory_space=pltpu.HBM)
+    ids_t = expert_ids.T
+    ins = (
+        layer_input,
+        output_grad,
+        latent_saved,
+        combined_saved,
+        ids_t,
+        gate_values.T,
+        up_proj,
+        expert_in[0].T,
+        expert_out[0],
+    )
+    between = pl.pallas_call(
         functools.partial(fused_kernel, groups, shares, pad),
         out_shape=(
-            jax.ShapeDtypeStruct((tokens, width), BF16),
+            jax.ShapeDtypeStruct((slots, tokens), BF16),
+            jax.ShapeDtypeStruct((slots, ff), BF16),
+            jax.ShapeDtypeStruct((slots, ff), BF16),
+            jax.ShapeDtypeStruct((slots, latent), BF16),
+            jax.ShapeDtypeStruct((slots, latent), BF16),
+            jax.ShapeDtypeStruct((slots, wide), BF16),
+            jax.ShapeDtypeStruct((groups, slots, lw), BF16),
+            jax.ShapeDtypeStruct((groups, slots, width), BF16),
             jax.ShapeDtypeStruct((lw, width), F32),
-            jax.ShapeDtypeStruct((lw, width), F32),
-            jax.ShapeDtypeStruct(expert_ids.shape, F32),
-            jax.ShapeDtypeStruct(expert_in.shape, F32),
-            jax.ShapeDtypeStruct(expert_out.shape, F32),
         ),
-        in_specs=[vmem] * 10,
-        out_specs=[vmem] * 6,
-        scratch_shapes=[
-            pltpu.VMEM((tokens, slots), BF16),
+        in_specs=[hbm] * len(ins),
+        out_specs=[vmem] * 9,
+        scratch_shapes=[pltpu.VMEM(a.shape, a.dtype) for a in ins]
+        + [
             pltpu.VMEM((groups, pad, width), BF16),
             pltpu.VMEM((groups, pad, width), BF16),
             pltpu.VMEM((groups, pad, wide), BF16),
             pltpu.VMEM((groups, pad, wide), BF16),
             pltpu.VMEM((groups, pad, width), BF16),
-            pltpu.VMEM((groups, slots, width), BF16),
             pltpu.VMEM((groups - 1, lw, width), BF16),
             pltpu.VMEM((groups - 1, lw, width), BF16),
             pltpu.VMEM((slots, latent), F32),
             pltpu.VMEM((slots, latent), BF16),
             pltpu.VMEM((shares, block, latent), BF16),
-            pltpu.VMEM((slots, latent), BF16),
             pltpu.VMEM((slots, wide), F32),
             pltpu.VMEM((slots, wide), BF16),
             pltpu.VMEM((shares, block, wide), BF16),
             pltpu.VMEM((slots, wide), BF16),
-            pltpu.VMEM((slots, wide), BF16),
-            pltpu.VMEM((groups, slots, lw), BF16),
+            pltpu.SemaphoreType.DMA((len(ins),)),
             pltpu.SemaphoreType.DMA((6, 2, groups)),
             pltpu.SemaphoreType.DMA((4, 2, shares)),
         ],
         compiler_params=pltpu.CompilerParams(
-            collective_id=0, has_side_effects=True, vmem_limit_bytes=48 * 1024 * 1024
+            collective_id=0, has_side_effects=True, vmem_limit_bytes=60 * 1024 * 1024
         ),
-    )(
-        layer_input,
-        output_grad,
-        latent_saved,
-        combined_saved,
-        expert_ids,
-        gate_values,
-        down_proj,
-        up_proj,
-        expert_in[0],
-        expert_out[0],
-    )
+    )(*ins)
+    outs = (
+        jax.ShapeDtypeStruct((tokens, width), BF16),
+        jax.ShapeDtypeStruct((lw, width), F32),
+        jax.ShapeDtypeStruct((lw, width), F32),
+        jax.ShapeDtypeStruct(ids_t.shape, F32),
+        jax.ShapeDtypeStruct((ff, latent), F32),
+        jax.ShapeDtypeStruct((ff, latent), F32),
+    )
+    input_grad, down_grad, up_grad, gate_grad, in_grad, out_grad = pl.pallas_call(
+        functools.partial(outputs_kernel, groups, pad),
+        out_shape=outs,
+        in_specs=[vmem] * 11,
+        out_specs=[hbm] * 6,
+        scratch_shapes=[
+            pltpu.VMEM(outs[n].shape, outs[n].dtype) for n in (0, 1, 3, 4, 5)
+        ]
+        + [pltpu.SemaphoreType.DMA((6,))],
+        compiler_params=pltpu.CompilerParams(vmem_limit_bytes=56 * 1024 * 1024),
+    )(*between, ids_t, down_proj)
+    return (input_grad, down_grad, up_grad, gate_grad.T, in_grad.T[None], out_grad[None])
 
 
 def padded_rows(tokens):

time: 69.3 us -> 53.3 us (0.77)
  local copies, waits for them, and re-layouts: 18.1 us -> 0 us
  Pallas kernels: 50 us -> 52.5 us
    unnamed x29 -> x0, local copies, waits for them, and re-layouts: 13.5 us -> none
    pallas_call x2 -> x0, local copies, waits for them, and re-layouts: 4.58 us -> none  [fused(): pl.pallas_call(functools.partial(fused_kernel, groups, shares, pad), out_...]
    pallas_call x0 -> x1, Pallas kernels: none -> 4.19 us  [fused(): pl.pallas_call(functools.partial(outputs_kernel, groups, pad), out_shape=...]
    pallas_call x1, Pallas kernels: 50 us -> 48.3 us  [fused(): pl.pallas_call(functools.partial(fused_kernel, groups, shares, pad), out_...]
where the time goes in v2:
time: 53.3 us; the launch traced here: 53.1 us
  Pallas kernels  52.5 us (98%)
  between operations  0.64 us (1%)
    pallas_call x1, Pallas kernels, fused(): pl.pallas_call(functools.partial(fused_kernel, groups, shares, pad), out_...  48.3 us
    pallas_call x1, Pallas kernels, fused(): pl.pallas_call(functools.partial(outputs_kernel, groups, pad), out_shape=...  4.19 us

profile of v2, /device:TPU:0, one launch (start us, length us, event | category | flops | bytes accessed | tf_op | source)
XLA Modules:
  0.0 53.1 jit_solution(9941902378036068309)
XLA Ops:
  0.6 48.3 %shard_map.145 = (bf16[128,256]{1,0:T(8,128)(2,1)}, bf16[128,336]{1,0:T(8,128)(2,1)}, bf16[128,336]{1,0:T(8,128)(2,1)}, bf16[128,1024]{1,0:T(8,128)(2,1)}, bf16[...) custom-call(bf16[256,512]{1,0:T(8,128)(2,1)} %x_hbm.1, ...), custom_call_target="tpu_custom_call" | custom-call | tf_op jit(solution)/shard_map/pallas_call | solution.py:378
  48.9 4.2 %shard_map.146 = (bf16[256,512]{1,0:T(8,128)(2,1)}, f32[256,512]{1,0:T(8,128)}, f32[256,512]{1,0:T(8,128)}, f32[22,256]{1,0:T(8,128)}, f32[336,1024]{1,0:T(8,128)}, /*index=5*/f32[336,1024]{1,0:T(8,128)}) custom-call(bf16[128,256]{1,0:T(8,128)(2,1)} %get-tuple-element.21.disp_ref, bf16[128,336]{1,0:T(8,128)(2,1)} %get-tuple-element.22.scaled_ref, ...), custom_call_target="tpu_custom_call" | custom-call | tf_op jit(solution)/shard_map/pallas_call | solution.py:425

commit v3 on v2

--- a/solution.py
+++ b/solution.py
@@ -60,9 +60,11 @@
     up_s,
     up_r,
     cf,
+    ch,
     cs,
     cr,
     bf,
+    bh,
     bs,
     br,
     bag,
@@ -81,14 +83,16 @@
     def expert_peer(j):
         return lax.rem(e + j, groups)
 
-    def hidden_peer(j):
-        return lax.rem(h + j, shares)
-
-    def expert_source(j):
-        return lax.rem(e + (groups - j), groups)
-
-    def hidden_source(j):
-        return lax.rem(h + (shares - j), shares)
+    pairs = shares // 2
+    core = lax.rem(h, 2)
+    line = h // 2
+    sibling = line * 2 + 1 - core
+
+    def line_peer(j):
+        return lax.rem(line + j, pairs)
+
+    def line_source(j):
+        return lax.rem(line + (pairs - j), pairs)
 
     def to_expert(phase, j, src, dst):
         copy = pltpu.make_async_remote_copy(
@@ -102,17 +106,50 @@
         copy.start()
         return copy
 
-    def to_hidden(phase, j, src, dst):
+    def to_hidden(phase, j, peer, src, dst):
         copy = pltpu.make_async_remote_copy(
             src_ref=src,
             dst_ref=dst,
             send_sem=sems_h.at[phase, 0, j],
             recv_sem=sems_h.at[phase, 1, j],
-            device_id=(e, hidden_peer(j)),
+            device_id=(e, peer),
             device_id_type=pl.DeviceIdType.MESH,
         )
         copy.start()
         return copy
+
+    def swap_halves(phase, full, half):
+        return to_hidden(phase, 0, sibling, full.at[:, 1 - core], half)
+
+    def scatter_start(phase, swap, full, half, sends, lands):
+        swap.wait_recv()
+        sends[...] = (full[:, core] + half[...]).astype(BF16)
+        return [
+            to_hidden(
+                phase, j, line_peer(j) * 2 + core, sends.at[line_peer(j)], lands.at[line]
+            )
+            for j in range(1, pairs)
+        ]
+
+    def scatter_sums(copies, full, half, lands):
+        total = full[line, core] + half[line]
+        for j in range(1, pairs):
+            copies[j - 1].wait_recv()
+            total = total + lands[line_source(j)].astype(F32)
+        return total.astype(BF16)
+
+    def gather_blocks(phase, full):
+        mine = full.at[rows_at(h, block)]
+        copies = [
+            to_hidden(phase, j, line_peer(j) * 2 + core, mine, mine)
+            for j in range(1, pairs)
+        ]
+        shared = [to_hidden(phase + 1, 0, sibling, mine, mine)]
+        for j in range(1, pairs):
+            copies[j - 1].wait_recv()
+            theirs = full.at[rows_at(line_source(j) * 2 + core, block)]
+            shared.append(to_hidden(phase + 1, j, sibling, theirs, theirs))
+        return copies, shared
 
     sources = (ids_hbm, gates_hbm, og_hbm, z_hbm, up_hbm, ein_hbm, x_hbm, u_hbm, eout_hbm)
     targets = (ids_ref, gates_ref, og_ref, z_ref, up_ref, ein_ref, x_ref, u_ref, eout_ref)
@@ -132,11 +169,11 @@
             device_id=(expert_peer(j), h),
             device_id_type=pl.DeviceIdType.MESH,
         )
-    for j in range(1, shares):
+    for peer in [sibling] + [line_peer(j) * 2 + core for j in range(1, pairs)]:
         pl.semaphore_signal(
             barrier,
             inc=1,
-            device_id=(e, hidden_peer(j)),
+            device_id=(e, peer),
             device_id_type=pl.DeviceIdType.MESH,
         )
 
@@ -168,7 +205,7 @@
     og_in.wait()
 
     og_s[...] = mm(disp, og_ref[...], 1, 0).astype(BF16).reshape(og_s.shape)
-    pl.semaphore_wait(barrier, groups + shares - 2)
+    pl.semaphore_wait(barrier, groups + pairs - 1)
     og_c = [
         to_expert(0, j, og_s.at[expert_peer(j)], og_r.at[e]) for j in range(1, groups)
     ]
@@ -195,12 +232,9 @@
         c.wait_recv()
     up_in.wait()
     cot_part = mm(og_r[...].reshape(slots, og_ref.shape[1]), up_ref[...], 1, 1)
-    cs[...] = cot_part.astype(BF16)
-    cf[...] = cot_part
-    crs = [
-        to_hidden(0, j, cs.at[rows_at(hidden_peer(j), block)], cr.at[h])
-        for j in range(1, shares)
-    ]
+    cf[...] = cot_part.reshape(cf.shape)
+    cot_swap = swap_halves(0, cf, ch)
+    crs = scatter_start(1, cot_swap, cf, ch, cs, cr)
     for c in z_c:
         c.wait_recv()
     x_c = [
@@ -215,16 +249,9 @@
     square = act * act
     scaled_ref[...] = (gate_b * square).astype(BF16)
     eout_in.wait()
-    cot = cf[rows_at(h, block), :]
-    for j in range(1, shares):
-        crs[j - 1].wait_recv()
-        cot = cot + cr[hidden_source(j)].astype(F32)
-    cag[rows_at(h, block), :] = cot.astype(BF16)
-    cagc = [
-        to_hidden(1, j, cag.at[rows_at(h, block)], cag.at[rows_at(h, block)])
-        for j in range(1, shares)
-    ]
-    for c in cagc:
+    cag[rows_at(h, block), :] = scatter_sums(crs, cf, ch, cr)
+    cagc, cags = gather_blocks(2, cag)
+    for c in cags:
         c.wait_recv()
 
     cotb = cag[...]
@@ -234,29 +261,18 @@
     pre_ref[...] = pre_grad
     part = mm(pre_grad, ein_ref[...], 1, 0)
     gate_wide = jnp.broadcast_to(gate_part, (slots, LANES))
-    bf[:, 0:latent] = part
-    bf[:, latent : latent + LANES] = gate_wide
-    bs[:, 0:latent] = part.astype(BF16)
-    bs[:, latent : latent + LANES] = gate_wide.astype(BF16)
-    brs = [
-        to_hidden(2, j, bs.at[rows_at(hidden_peer(j), block)], br.at[h])
-        for j in range(1, shares)
-    ]
-    total = bf[rows_at(h, block), :]
-    for j in range(1, shares):
-        brs[j - 1].wait_recv()
-        total = total + br[hidden_source(j)].astype(F32)
-    bag[rows_at(h, block), :] = total.astype(BF16)
-    bagc = [
-        to_hidden(3, j, bag.at[rows_at(h, block)], bag.at[rows_at(h, block)])
-        for j in range(1, shares)
-    ]
+    bf[:, :, :, 0:latent] = part.reshape(pairs, 2, block, latent)
+    bf[:, :, :, latent : latent + LANES] = gate_wide.reshape(pairs, 2, block, LANES)
+    back_swap = swap_halves(4, bf, bh)
+    brs = scatter_start(5, back_swap, bf, bh, bs, br)
+    bag[rows_at(h, block), :] = scatter_sums(brs, bf, bh, br)
+    bagc, bags = gather_blocks(6, bag)
     for j in range(1, groups):
         up_c[j - 1].wait_recv()
         ug_ref[...] += up_r[j - 1].astype(F32)
     for c in x_c:
         c.wait_recv()
-    for c in bagc:
+    for c in bags:
         c.wait_recv()
 
     home_c = [
@@ -271,7 +287,9 @@
     dn[e] = bag[:, rows_at(e, lw)]
     for c in home_c + dn_c:
         c.wait_recv()
-    for c in og_c + z_c + crs + x_c + up_c + cagc + brs + bagc + home_c + dn_c:
+    sent = og_c + z_c + [cot_swap] + crs + x_c + up_c + cagc + cags
+    sent += [back_swap] + brs + bagc + bags + home_c + dn_c
+    for c in sent:
         c.wait_send()
 
 
@@ -399,16 +417,18 @@
             pltpu.VMEM((groups, pad, width), BF16),
             pltpu.VMEM((groups - 1, lw, width), BF16),
             pltpu.VMEM((groups - 1, lw, width), BF16),
-            pltpu.VMEM((slots, latent), F32),
-            pltpu.VMEM((slots, latent), BF16),
-            pltpu.VMEM((shares, block, latent), BF16),
-            pltpu.VMEM((slots, wide), F32),
-            pltpu.VMEM((slots, wide), BF16),
-            pltpu.VMEM((shares, block, wide), BF16),
+            pltpu.VMEM((shares // 2, 2, block, latent), F32),
+            pltpu.VMEM((shares // 2, block, latent), F32),
+            pltpu.VMEM((shares // 2, block, latent), BF16),
+            pltpu.VMEM((shares // 2, block, latent), BF16),
+            pltpu.VMEM((shares // 2, 2, block, wide), F32),
+            pltpu.VMEM((shares // 2, block, wide), F32),
+            pltpu.VMEM((shares // 2, block, wide), BF16),
+            pltpu.VMEM((shares // 2, block, wide), BF16),
             pltpu.VMEM((slots, wide), BF16),
             pltpu.SemaphoreType.DMA((len(ins),)),
             pltpu.SemaphoreType.DMA((6, 2, groups)),
-            pltpu.SemaphoreType.DMA((4, 2, shares)),
+            pltpu.SemaphoreType.DMA((8, 2, shares // 2)),
         ],
         compiler_params=pltpu.CompilerParams(
             collective_id=0, has_side_effects=True, vmem_limit_bytes=60 * 1024 * 1024
@@ -446,6 +466,7 @@
     slots = groups * padded_rows(layer_input.shape[0])
     return (
         expert_in.shape[0] == 1
+        and shares % 2 == 0
         and slots % (ROWS * shares) == 0
         and slots % LANES == 0
         and latent_saved.shape[1] % (LANES * groups) == 0

time: 53.3 us -> 48.1 us (0.902)
  Pallas kernels: 52.5 us -> 47.3 us
    pallas_call x1, Pallas kernels: 48.3 us -> 43.2 us  [fused(): pl.pallas_call(functools.partial(fused_kernel, groups, shares, pad), out_...]
where the time goes in v3:
time: 48.1 us; the launch traced here: 48 us
  Pallas kernels  47.3 us (98%)
  between operations  0.64 us (1%)
    pallas_call x1, Pallas kernels, fused(): pl.pallas_call(functools.partial(fused_kernel, groups, shares, pad), out_...  43.2 us
    pallas_call x1, Pallas kernels, fused(): pl.pallas_call(functools.partial(outputs_kernel, groups, pad), out_shape=...  4.2 us

profile of v3, /device:TPU:0, one launch (start us, length us, event | category | flops | bytes accessed | tf_op | source)
XLA Modules:
  0.0 48.0 jit_solution(16725057829559631708)
XLA Ops:
  0.6 43.2 %shard_map.145 = (bf16[128,256]{1,0:T(8,128)(2,1)}, bf16[128,336]{1,0:T(8,128)(2,1)}, bf16[128,336]{1,0:T(8,128)(2,1)}, bf16[128,1024]{1,0:T(8,128)(2,1)}, bf16[...) custom-call(bf16[256,512]{1,0:T(8,128)(2,1)} %x_hbm.1, ...), custom_call_target="tpu_custom_call" | custom-call | tf_op jit(solution)/shard_map/pallas_call | solution.py:396
  43.8 4.2 %shard_map.146 = (bf16[256,512]{1,0:T(8,128)(2,1)}, f32[256,512]{1,0:T(8,128)}, f32[256,512]{1,0:T(8,128)}, f32[22,256]{1,0:T(8,128)}, f32[336,1024]{1,0:T(8,128)}, /*index=5*/f32[336,1024]{1,0:T(8,128)}) custom-call(bf16[128,256]{1,0:T(8,128)(2,1)} %get-tuple-element.21.disp_ref, bf16[128,336]{1,0:T(8,128)(2,1)} %get-tuple-element.22.scaled_ref, ...), custom_call_target="tpu_custom_call" | custom-call | tf_op jit(solution)/shard_map/pallas_call | solution.py:445

commit v4 on v3

--- a/solution.py
+++ b/solution.py
@@ -118,6 +118,21 @@
         copy.start()
         return copy
 
+    def to_sibling(phase, j, src, dst):
+        copy = pltpu.make_async_remote_copy(
+            src_ref=src,
+            dst_ref=dst,
+            send_sem=sems_e.at[phase, 0, j],
+            recv_sem=sems_e.at[phase, 1, j],
+            device_id=(e, sibling),
+            device_id_type=pl.DeviceIdType.MESH,
+        )
+        copy.start()
+        return copy
+
+    def expert_source(j):
+        return lax.rem(e + (groups - j), groups)
+
     def swap_halves(phase, full, half):
         return to_hidden(phase, 0, sibling, full.at[:, 1 - core], half)
 
@@ -215,7 +230,11 @@
     z_s[:, :, latent : latent + LANES] = (
         jnp.broadcast_to(gate_col, (slots, LANES)).astype(BF16).reshape(groups, pad, LANES)
     )
-    z_c = [to_expert(1, j, z_s.at[expert_peer(j)], z_r.at[e]) for j in range(1, groups)]
+    my_rows = rows_at(core, pad // 2)
+    z_c = [
+        to_expert(1, j, z_s.at[expert_peer(j), my_rows], z_r.at[e, my_rows])
+        for j in range(1, groups)
+    ]
     og_r[e] = og_s[e]
     z_r[e] = z_s[e]
     x_in.wait()
@@ -235,12 +254,17 @@
     cf[...] = cot_part.reshape(cf.shape)
     cot_swap = swap_halves(0, cf, ch)
     crs = scatter_start(1, cot_swap, cf, ch, cs, cr)
-    for c in z_c:
-        c.wait_recv()
+    z_f = []
+    for j in range(1, groups):
+        z_c[j - 1].wait_recv()
+        landed = z_r.at[expert_source(j), my_rows]
+        z_f.append(to_sibling(6, j, landed, landed))
     x_c = [
         to_expert(2, j, x_s, x_r.at[:, rows_at(e, pad), :]) for j in range(1, groups)
     ]
     up_c = [to_expert(3, j, up_s.at[j - 1], up_r.at[j - 1]) for j in range(1, groups)]
+    for c in z_f:
+        c.wait_recv()
     zb = z_r[:, :, 0:latent].reshape(slots, latent)
     gate_b = z_r[:, :, latent : latent + LANES].astype(F32).reshape(slots, LANES)[:, 0:1]
     zb_ref[...] = zb
@@ -275,20 +299,36 @@
     for c in bags:
         c.wait_recv()
 
+    half_pad = pad // 2
+    my_half = rows_at(core, slots // 2)
     home_c = [
-        to_expert(4, j, bag.at[rows_at(expert_peer(j), pad)], home.at[rows_at(e, pad)])
+        to_expert(
+            4,
+            j,
+            bag.at[rows_at(expert_peer(j) * 2 + core, half_pad)],
+            home.at[rows_at(e * 2 + core, half_pad)],
+        )
         for j in range(1, groups)
     ]
     dn_c = [
-        to_expert(5, j, bag.at[:, rows_at(expert_peer(j), lw)], dn.at[e])
+        to_expert(5, j, bag.at[my_half, rows_at(expert_peer(j), lw)], dn.at[e, my_half])
         for j in range(1, groups)
     ]
     home[rows_at(e, pad), :] = bag[rows_at(e, pad), :]
     dn[e] = bag[:, rows_at(e, lw)]
-    for c in home_c + dn_c:
+    last_f = []
+    for j in range(1, groups):
+        home_c[j - 1].wait_recv()
+        landed = home.at[rows_at(expert_source(j) * 2 + core, half_pad)]
+        last_f.append(to_sibling(7, j, landed, landed))
+    for j in range(1, groups):
+        dn_c[j - 1].wait_recv()
+        landed = dn.at[expert_source(j), my_half]
+        last_f.append(to_sibling(8, j, landed, landed))
+    for c in last_f:
         c.wait_recv()
     sent = og_c + z_c + [cot_swap] + crs + x_c + up_c + cagc + cags
-    sent += [back_swap] + brs + bagc + bags + home_c + dn_c
+    sent += [back_swap] + brs + bagc + bags + home_c + dn_c + z_f + last_f
     for c in sent:
         c.wait_send()
 
@@ -296,30 +336,32 @@
 def outputs_kernel(
     groups,
     pad,
-    disp_ref,
-    scaled_ref,
-    pre_ref,
-    zb_ref,
-    cot_ref,
-    home_ref,
-    dn_ref,
-    x_ref,
-    ug_ref,
-    ids_ref,
-    down_ref,
-    ig_hbm,
-    dg_hbm,
-    ug_hbm,
-    gg_hbm,
-    eig_hbm,
-    eog_hbm,
-    ig_v,
-    dg_v,
-    gg_v,
-    eig_v,
-    eog_v,
-    sems,
+    *refs,
 ):
+    sources, refs = refs[:11], refs[11:]
+    (ig_hbm, dg_hbm, ug_hbm, gg_hbm, eig_hbm, eog_hbm), refs = refs[:6], refs[6:]
+    targets, refs = refs[:11], refs[11:]
+    ig_v, dg_v, gg_v, eig_v, eog_v, sems, sems_in = refs
+    (
+        disp_ref,
+        scaled_ref,
+        pre_ref,
+        zb_ref,
+        cot_ref,
+        home_ref,
+        dn_ref,
+        x_ref,
+        ug_ref,
+        ids_ref,
+        down_ref,
+    ) = targets
+    loads = [
+        pltpu.make_async_copy(src, dst, sems_in.at[n])
+        for n, (src, dst) in enumerate(zip(sources, targets))
+    ]
+    order = (1, 4, 2, 3, 8, 6, 7, 0, 5, 10, 9)
+    for n in order:
+        loads[n].start()
     slots = groups * pad
     latent = cot_ref.shape[1]
     stores = []
@@ -329,11 +371,18 @@
         copy.start()
         stores.append(copy)
 
-    store(ug_ref, ug_hbm)
+    loads[1].wait()
+    loads[4].wait()
     eog_v[...] = mm(scaled_ref[...], cot_ref[...], 0, 0)
     store(eog_v, eog_hbm)
+    loads[2].wait()
+    loads[3].wait()
     eig_v[...] = mm(pre_ref[...], zb_ref[...], 0, 0)
     store(eig_v, eig_hbm)
+    loads[8].wait()
+    store(ug_ref, ug_hbm)
+    loads[6].wait()
+    loads[7].wait()
     dg_v[...] = mm(
         dn_ref[...].reshape(groups * slots, dn_ref.shape[2]),
         x_ref[...].reshape(groups * slots, x_ref.shape[2]),
@@ -341,6 +390,8 @@
         0,
     )
     store(dg_v, dg_hbm)
+    for n in (0, 5, 10, 9):
+        loads[n].wait()
     disp = disp_ref[...]
     latent_grad = mm(disp, home_ref[:, 0:latent], 0, 0).astype(BF16)
     ig_v[...] = mm(latent_grad, down_ref[...], 1, 0).astype(BF16)
@@ -427,7 +478,7 @@
             pltpu.VMEM((shares // 2, block, wide), BF16),
             pltpu.VMEM((slots, wide), BF16),
             pltpu.SemaphoreType.DMA((len(ins),)),
-            pltpu.SemaphoreType.DMA((6, 2, groups)),
+            pltpu.SemaphoreType.DMA((9, 2, groups)),
             pltpu.SemaphoreType.DMA((8, 2, shares // 2)),
         ],
         compiler_params=pltpu.CompilerParams(
@@ -445,19 +496,22 @@
     input_grad, down_grad, up_grad, gate_grad, in_grad, out_grad = pl.pallas_call(
         functools.partial(outputs_kernel, groups, pad),
         out_shape=outs,
-        in_specs=[vmem] * 11,
+        in_specs=[hbm] * 11,
         out_specs=[hbm] * 6,
         scratch_shapes=[
+            pltpu.VMEM(a.shape, a.dtype) for a in (*between, ids_t, down_proj)
+        ]
+        + [
             pltpu.VMEM(outs[n].shape, outs[n].dtype) for n in (0, 1, 3, 4, 5)
         ]
-        + [pltpu.SemaphoreType.DMA((6,))],
-        compiler_params=pltpu.CompilerParams(vmem_limit_bytes=56 * 1024 * 1024),
+        + [pltpu.SemaphoreType.DMA((6,)), pltpu.SemaphoreType.DMA((11,))],
+        compiler_params=pltpu.CompilerParams(vmem_limit_bytes=60 * 1024 * 1024),
     )(*between, ids_t, down_proj)
     return (input_grad, down_grad, up_grad, gate_grad.T, in_grad.T[None], out_grad[None])
 
 
 def padded_rows(tokens):
-    return -(-(tokens * 3 // 32) // ROWS) * ROWS
+    return -(-(tokens * 3 // 32) // (2 * ROWS)) * 2 * ROWS
 
 
 def fits(layer_input, latent_saved, expert_in):

time: 48.1 us -> 45.7 us (0.950)
  Pallas kernels: 47.3 us -> 44.9 us
    pallas_call x1, Pallas kernels: 43.2 us -> 41.4 us  [fused(): pl.pallas_call(functools.partial(fused_kernel, groups, shares, pad), out_...]
    pallas_call x1, Pallas kernels: 4.2 us -> 3.52 us  [fused(): pl.pallas_call(functools.partial(outputs_kernel, groups, pad), out_shape=...]
where the time goes in v4:
time: 45.7 us; the launch traced here: 45.5 us
  Pallas kernels  44.9 us (98%)
  between operations  0.64 us (1%)
    pallas_call x1, Pallas kernels, fused(): pl.pallas_call(functools.partial(fused_kernel, groups, shares, pad), out_...  41.4 us
    pallas_call x1, Pallas kernels, fused(): pl.pallas_call(functools.partial(outputs_kernel, groups, pad), out_shape=...  3.52 us

profile of v4, /device:TPU:0, one launch (start us, length us, event | category | flops | bytes accessed | tf_op | source)
XLA Modules:
  0.0 45.5 jit_solution(6441045468315656956)
XLA Ops:
  0.6 41.4 %shard_map.145 = (bf16[128,256]{1,0:T(8,128)(2,1)}, bf16[128,336]{1,0:T(8,128)(2,1)}, bf16[128,336]{1,0:T(8,128)(2,1)}, bf16[128,1024]{1,0:T(8,128)(2,1)}, bf16[...) custom-call(bf16[256,512]{1,0:T(8,128)(2,1)} %x_hbm.1, ...), custom_call_target="tpu_custom_call" | custom-call | tf_op jit(solution)/shard_map/pallas_call | solution.py:447
  42.0 3.5 %shard_map.146 = (bf16[256,512]{1,0:T(8,128)(2,1)}, f32[256,512]{1,0:T(8,128)}, f32[256,512]{1,0:T(8,128)}, f32[22,256]{1,0:T(8,128)}, f32[336,1024]{1,0:T(8,128)}, /*index=5*/f32[336,1024]{1,0:T(8,128)}) custom-call(bf16[128,256]{1,0:T(8,128)(2,1)} %get-tuple-element.21.refs_0_, bf16[128,336]{1,0:T(8,128)(2,1)} %get-tuple-element.22.refs_1_, ...), custom_call_target="tpu_custom_call" | custom-call | tf_op jit(solution)/shard_map/pallas_call | solution.py:496

commit v5 on v4

--- a/solution.py
+++ b/solution.py
@@ -34,6 +34,15 @@
     up_hbm,
     ein_hbm,
     eout_hbm,
+    disp_out,
+    scaled_out,
+    pre_out,
+    zb_out,
+    cag_out,
+    home_out,
+    dn_out,
+    x_out,
+    ug_out,
     disp_ref,
     scaled_ref,
     pre_ref,
@@ -69,6 +78,7 @@
     br,
     bag,
     sems_in,
+    sems_out,
     sems_e,
     sems_h,
 ):
@@ -165,6 +175,13 @@
             theirs = full.at[rows_at(line_source(j) * 2 + core, block)]
             shared.append(to_hidden(phase + 1, j, sibling, theirs, theirs))
         return copies, shared
+
+    stores = []
+
+    def store(src, dst):
+        copy = pltpu.make_async_copy(src, dst, sems_out.at[len(stores)])
+        copy.start()
+        stores.append(copy)
 
     sources = (ids_hbm, gates_hbm, og_hbm, z_hbm, up_hbm, ein_hbm, x_hbm, u_hbm, eout_hbm)
     targets = (ids_ref, gates_ref, og_ref, z_ref, up_ref, ein_ref, x_ref, u_ref, eout_ref)
@@ -288,14 +305,14 @@
     bf[:, :, :, 0:latent] = part.reshape(pairs, 2, block, latent)
     bf[:, :, :, latent : latent + LANES] = gate_wide.reshape(pairs, 2, block, LANES)
     back_swap = swap_halves(4, bf, bh)
+    store(disp_ref, disp_out)
+    store(scaled_ref, scaled_out)
+    store(pre_ref, pre_out)
+    store(zb_ref, zb_out)
+    store(cag, cag_out)
     brs = scatter_start(5, back_swap, bf, bh, bs, br)
     bag[rows_at(h, block), :] = scatter_sums(brs, bf, bh, br)
     bagc, bags = gather_blocks(6, bag)
-    for j in range(1, groups):
-        up_c[j - 1].wait_recv()
-        ug_ref[...] += up_r[j - 1].astype(F32)
-    for c in x_c:
-        c.wait_recv()
     for c in bags:
         c.wait_recv()
 
@@ -316,6 +333,13 @@
     ]
     home[rows_at(e, pad), :] = bag[rows_at(e, pad), :]
     dn[e] = bag[:, rows_at(e, lw)]
+    for j in range(1, groups):
+        up_c[j - 1].wait_recv()
+        ug_ref[...] += up_r[j - 1].astype(F32)
+    for c in x_c:
+        c.wait_recv()
+    store(ug_ref, ug_out)
+    store(x_r, x_out)
     last_f = []
     for j in range(1, groups):
         home_c[j - 1].wait_recv()
@@ -327,6 +351,10 @@
         last_f.append(to_sibling(8, j, landed, landed))
     for c in last_f:
         c.wait_recv()
+    store(home, home_out)
+    store(dn, dn_out)
+    for c in stores:
+        c.wait()
     sent = og_c + z_c + [cot_swap] + crs + x_c + up_c + cagc + cags
     sent += [back_swap] + brs + bagc + bags + home_c + dn_c + z_f + last_f
     for c in sent:
@@ -430,7 +458,6 @@
     block = slots // shares
     wide = latent + LANES
     lw = latent // groups
-    vmem = pl.BlockSpec(memory_space=pltpu.VMEM)
     hbm = pl.BlockSpec(memory_space=pltpu.HBM)
     ids_t = expert_ids.T
     ins = (
@@ -444,22 +471,23 @@
         expert_in[0].T,
         expert_out[0],
     )
+    middle = (
+        jax.ShapeDtypeStruct((slots, tokens), BF16),
+        jax.ShapeDtypeStruct((slots, ff), BF16),
+        jax.ShapeDtypeStruct((slots, ff), BF16),
+        jax.ShapeDtypeStruct((slots, latent), BF16),
+        jax.ShapeDtypeStruct((slots, latent), BF16),
+        jax.ShapeDtypeStruct((slots, wide), BF16),
+        jax.ShapeDtypeStruct((groups, slots, lw), BF16),
+        jax.ShapeDtypeStruct((groups, slots, width), BF16),
+        jax.ShapeDtypeStruct((lw, width), F32),
+    )
     between = pl.pallas_call(
         functools.partial(fused_kernel, groups, shares, pad),
-        out_shape=(
-            jax.ShapeDtypeStruct((slots, tokens), BF16),
-            jax.ShapeDtypeStruct((slots, ff), BF16),
-            jax.ShapeDtypeStruct((slots, ff), BF16),
-            jax.ShapeDtypeStruct((slots, latent), BF16),
-            jax.ShapeDtypeStruct((slots, latent), BF16),
-            jax.ShapeDtypeStruct((slots, wide), BF16),
-            jax.ShapeDtypeStruct((groups, slots, lw), BF16),
-            jax.ShapeDtypeStruct((groups, slots, width), BF16),
-            jax.ShapeDtypeStruct((lw, width), F32),
-        ),
+        out_shape=middle,
         in_specs=[hbm] * len(ins),
-        out_specs=[vmem] * 9,
-        scratch_shapes=[pltpu.VMEM(a.shape, a.dtype) for a in ins]
+        out_specs=[hbm] * len(middle),
+        scratch_shapes=[pltpu.VMEM(a.shape, a.dtype) for a in middle + ins]
         + [
             pltpu.VMEM((groups, pad, width), BF16),
             pltpu.VMEM((groups, pad, width), BF16),
@@ -478,6 +506,7 @@
             pltpu.VMEM((shares // 2, block, wide), BF16),
             pltpu.VMEM((slots, wide), BF16),
             pltpu.SemaphoreType.DMA((len(ins),)),
+            pltpu.SemaphoreType.DMA((len(middle),)),
             pltpu.SemaphoreType.DMA((9, 2, groups)),
             pltpu.SemaphoreType.DMA((8, 2, shares // 2)),
         ],

time: 45.7 us -> 45 us (0.985)
  Pallas kernels: 44.9 us -> 44.2 us
    pallas_call x1, Pallas kernels: 41.4 us -> 40.7 us  [fused(): pl.pallas_call(functools.partial(fused_kernel, groups, shares, pad), out_...]
where the time goes in v5:
time: 45 us; the launch traced here: 44.8 us
  Pallas kernels  44.2 us (98%)
  between operations  0.64 us (1%)
    pallas_call x1, Pallas kernels, fused(): pl.pallas_call(functools.partial(fused_kernel, groups, shares, pad), out_...  40.7 us
    pallas_call x1, Pallas kernels, fused(): pl.pallas_call(functools.partial(outputs_kernel, groups, pad), out_shape=...  3.51 us

profile of v5, /device:TPU:0, one launch (start us, length us, event | category | flops | bytes accessed | tf_op | source)
XLA Modules:
  0.0 44.8 jit_solution(13665113753809050654)
XLA Ops:
  0.6 40.7 %shard_map.145 = (bf16[128,256]{1,0:T(8,128)(2,1)}, bf16[128,336]{1,0:T(8,128)(2,1)}, bf16[128,336]{1,0:T(8,128)(2,1)}, bf16[128,1024]{1,0:T(8,128)(2,1)}, bf16[...) custom-call(bf16[256,512]{1,0:T(8,128)(2,1)} %x_hbm.1, ...), custom_call_target="tpu_custom_call" | custom-call | tf_op jit(solution)/shard_map/pallas_call | solution.py:485
  41.3 3.5 %shard_map.146 = (bf16[256,512]{1,0:T(8,128)(2,1)}, f32[256,512]{1,0:T(8,128)}, f32[256,512]{1,0:T(8,128)}, f32[22,256]{1,0:T(8,128)}, f32[336,1024]{1,0:T(8,128)}, /*index=5*/f32[336,1024]{1,0:T(8,128)}) custom-call(bf16[128,256]{1,0:T(8,128)(2,1)} %get-tuple-element.21.refs_0_, bf16[128,336]{1,0:T(8,128)(2,1)} %get-tuple-element.22.refs_1_, ...), custom_call_target="tpu_custom_call" | custom-call | tf_op jit(solution)/shard_map/pallas_call | solution.py:525
